TPU v7x, 512 devices: a whole 4x4x16 slice. The times are simulated.
512 devices in a mesh: space: 32 (over y_hi, z), rep: 16 (over y_lo, x, core).
Axes of the slice: x: 4, y: 4 (y_hi: 2, y_lo: 2; y = y_hi * 2 + y_lo), z: 16, core: 2. Of those that a mesh axis runs over, the one named last changes fastest.
Arguments:
- volumes: bfloat16 [16, 32, 8, 4, 16, 256], P('rep', 'space'), may hold values from -6 to 6
- grad_parts: bfloat16 [16, 2, 6912, 256], P('rep', None, 'space'), may hold values from -6 to 6
- master_weights: float32 [2, 6912, 256], P(None, 'space'), may hold values from -0.078125 to 0.078125
- moment_first: float32 [16, 2, 6912, 256], P('rep', None, 'space'), may hold values from -12 to 12
- moment_second: float32 [16, 2, 6912, 256], P('rep', None, 'space'), may hold values from 1 to 30
- owner: int32 [2, 32], replicated, may hold values from 0 to 15
Outputs:
- features: bfloat16 [16, 32, 8, 4, 16, 256], P('rep', 'space')
- new_weights: float32 [2, 1769472], P(None, ('space', 'rep'))
- moment_first_out: float32 [16, 2, 6912, 256], P('rep', None, 'space')
- moment_second_out: float32 [16, 2, 6912, 256], P('rep', None, 'space')
Inputs may be any that keep to these rules, and one draw needn't show every extreme that they name: owner[f, p] is the replica whose state slot holds the optimizer state of panel p of filter f, rows p * 216 to (p + 1) * 216 - 1; replicas may own unequal numbers of panels.
All inputs are finite; a program needn't handle non-finite values.
Results may differ from a plain program's by a relative error of at most 0.0095.
Values may be sent and summed in bfloat16 or wider, within the bound.
A program may use at most 64 MiB of HBM per device.

v0:
```python
import jax
import jax.numpy as jnp
from jax import lax
from jax.sharding import PartitionSpec as P

GY = 2
GZ = 2
PANEL_ROWS = 216


def passed_along(value, axis, steps):
    count = lax.axis_size(axis)
    first, last = (max(0, -steps), min(count, count - steps))
    return lax.ppermute(value, axis, [(source, source + steps) for source in range(first, last)])


def over_pieces(array, axis):
    blocks = lax.all_gather(array, axis).astype(jnp.float32)
    return blocks.sum(axis=0)


def from_root(array, axis, root):
    return lax.dynamic_index_in_dim(lax.all_gather(array, axis), root, 0, keepdims=False)


def neighbour(slab, offset):
    return passed_along(slab, "space", offset)


def keep_when(flag, slab):
    return jnp.where(flag, slab, jnp.zeros_like(slab))


def side_slab(array, dim, side):
    length = array.shape[dim]
    if side < 0:
        return lax.slice_in_dim(array, length - 1, length, 1, dim)
    return lax.slice_in_dim(array, 0, 1, 1, dim)


def extend_brick(brick, coords, strides, grid):
    lows = [coords[d] > 0 for d in range(3)]
    highs = [coords[d] < grid[d] - 1 for d in range(3)]
    current = brick
    for dim in range(3):
        lower = keep_when(lows[dim], neighbour(side_slab(current, dim, -1), strides[dim]))
        upper = keep_when(highs[dim], neighbour(side_slab(current, dim, 1), -strides[dim]))
        current = jnp.concatenate([lower, current, upper], axis=dim)
    return current


def convolve(extended, filter_rows):
    extent_x = extended.shape[0] - 2
    extent_y = extended.shape[1] - 2
    extent_z = extended.shape[2] - 2
    channels = extended.shape[3]
    summed = jnp.zeros((extent_x * extent_y * extent_z, filter_rows.shape[1]), jnp.float32)
    for shift_x in range(3):
        for shift_y in range(3):
            for shift_z in range(3):
                tap_index = (shift_x * 3 + shift_y) * 3 + shift_z
                window = extended[
                    shift_x : shift_x + extent_x,
                    shift_y : shift_y + extent_y,
                    shift_z : shift_z + extent_z,
                ]
                weights_tap = filter_rows[tap_index * channels : (tap_index + 1) * channels]
                summed = summed + jnp.dot(
                    window.reshape(-1, channels), weights_tap, preferred_element_type=jnp.float32
                )
    return summed.reshape(extent_x, extent_y, extent_z, -1)


def shards(volumes, grad_parts, master_weights, moment_first, moment_second, owner):
    filter_count = master_weights.shape[0]
    rows_dev = master_weights.shape[1]
    channels = master_weights.shape[2]
    panels_dev = rows_dev // PANEL_ROWS
    space_pos = lax.axis_index("space")
    rep_pos = lax.axis_index("rep")
    summed_grad = over_pieces(grad_parts[0].astype(jnp.float32).astype(jnp.bfloat16), "rep").astype(
        jnp.float32
    )
    first_new = 0.9 * moment_first[0] + 0.1 * summed_grad
    second_new = 0.95 * moment_second[0] + 0.05 * (summed_grad * summed_grad)
    owner_local = lax.dynamic_slice_in_dim(owner, space_pos * panels_dev, panels_dev, 1)
    owner_rows = jnp.repeat(owner_local, PANEL_ROWS, axis=1)
    owned = (owner_rows == rep_pos)[:, :, None]
    first_out = jnp.where(owned, first_new, moment_first[0])[None]
    second_out = jnp.where(owned, second_new, moment_second[0])[None]
    corr_one = 1.0 - 0.9**10
    corr_two = 1.0 - 0.95**10
    update = first_new / corr_one / (jnp.sqrt(second_new / corr_two) + 1e-08) + 0.1 * master_weights
    candidate = master_weights - 0.004 * update
    per_filter = []
    for filter_index in range(filter_count):
        slab = candidate[filter_index, 0:PANEL_ROWS]
        slabs = from_root(slab.astype(jnp.bfloat16), "rep", owner_local[filter_index, 0]).astype(
            slab.dtype
        )
        per_filter.append(slabs)
    new_master = jnp.stack(per_filter)
    share_len = rows_dev * channels // lax.axis_size("rep")
    new_weights = lax.dynamic_slice_in_dim(
        new_master.reshape(filter_count, -1), rep_pos * share_len, share_len, 1
    )
    filters = lax.all_gather(new_master.astype(jnp.bfloat16), "space", axis=1, tiled=True)
    grid = (lax.axis_size("space") // (GY * GZ), GY, GZ)
    strides = (GY * GZ, GZ, 1)
    coords = (space_pos // (GY * GZ), space_pos // GZ % GY, space_pos % GZ)
    brick = volumes[0, 0]
    hidden = jax.nn.gelu(
        convolve(extend_brick(brick, coords, strides, grid), filters[0]), approximate=True
    ).astype(jnp.bfloat16)
    output = jax.nn.gelu(
        convolve(extend_brick(hidden, coords, strides, grid), filters[1]), approximate=True
    ).astype(jnp.bfloat16)
    return (output[None, None], new_weights, first_out, second_out)


def solution(mesh):
    placed = (
        P("rep", "space", None, None, None, None),
        P("rep", None, "space", None),
        P(None, "space", None),
        P("rep", None, "space", None),
        P("rep", None, "space", None),
        P(),
    )
    return jax.shard_map(
        shards,
        mesh=mesh,
        in_specs=placed,
        out_specs=(
            P("rep", "space", None, None, None, None),
            P(None, ("space", "rep")),
            P("rep", None, "space", None),
            P("rep", None, "space", None),
        ),
        check_vma=False,
    )
```

profile of v0, /device:TPU:24, one launch (start us, length us, event | category | flops | bytes accessed | tf_op | source)
XLA Modules:
  0.0 415.0 jit_solution(16245634699472826510)
XLA Ops:
  8.0 50.1 %all-gather.5.cloned.1.call-done = bf16[16,2,216,256]{3,2,1,0:T(8,128)(2,1)} async-done(((bf16[1,2,216,256]{3,2,1,0:T(8,128)(2,1)}), bf16[16,2,216,256]{3,2,1,0:T(8,128)(2,1)}) %all-gather.5.cloned.1.call-update) | async-done | bytes 3538960 | tf_op jit(solution)/shard_map/all_gather | solution.py:18
  58.1 2.6 convert_reduce_fusion
  69.1 35.6 %all-gather.9.cloned.1.call-done = bf16[16,216,256]{2,1,0:T(8,128)(2,1)} async-done(((bf16[1,216,256]{2,1,0:T(8,128)(2,1)}), bf16[16,216,256]{2,1,0:T(8,128)(2,1)}) %all-gather.9.cloned.1.call-update) | async-done | bytes 1769488 | tf_op jit(solution)/shard_map/all_gather | solution.py:23
  105.6 43.1 %all-gather.7.cloned.1.call-done = bf16[16,216,256]{2,1,0:T(8,128)(2,1)} async-done(((bf16[1,216,256]{2,1,0:T(8,128)(2,1)}), bf16[16,216,256]{2,1,0:T(8,128)(2,1)}) %all-gather.7.cloned.1.call-update) | async-done | bytes 1769488 | tf_op jit(solution)/shard_map/all_gather | solution.py:23
  150.3 7.6 %collective-permute-start = (bf16[1,4,16,256]{3,2,1,0:T(8,128)(2,1)S(1)}, bf16[1,4,16,256]{3,2,1,0:T(8,128)(2,1)S(1)}, u32[]{:S(2)}, u32[]{:S(2)}) collective-permute-start(bf16[1,4,16,256]{3,2,1,0:T(8,128)(2,1)S(1)} %get-tuple-element.78), channel_id=1, source_target_pairs={{0,64},{16,80},{32,96},{48,112},{64,128},{80,144},{96,160},{112,17... | collective-permute-start | bytes 98312 | tf_op jit(solution)/shard_map/ppermute | solution.py:14
  158.0 4.5 %collective-permute-start.1 = (bf16[1,4,16,256]{3,2,1,0:T(8,128)(2,1)S(1)}, bf16[1,4,16,256]{3,2,1,0:T(8,128)(2,1)S(1)}, u32[]{:S(2)}, u32[]{:S(2)}) collective-permute-start(bf16[1,4,16,256]{3,2,1,0:T(8,128)(2,1)S(1)} %get-tuple-element.79), channel_id=1, source_target_pairs={{64,0},{80,16},{96,32},{112,48},{128,64},{144,80},{160,96},{176,11... | collective-permute-start | bytes 98312 | tf_op jit(solution)/shard_map/ppermute | solution.py:14
  162.6 5.5 %collective-permute-done.1 = bf16[1,4,16,256]{3,2,1,0:T(8,128)(2,1)S(1)} collective-permute-done((bf16[1,4,16,256]{3,2,1,0:T(8,128)(2,1)S(1)}, bf16[1,4,16,256]{3,2,1,0:T(8,128)(2,1)S(1)}, u32[]{:S(2)}, u32[]{:S(2)}) %collective-permute-start.1) | collective-permute-done | bytes 32800 | tf_op jit(solution)/shard_map/ppermute | solution.py:14
  168.1 4.4 %collective-permute-start.2 = (bf16[10,1,16,256]{3,2,1,0:T(8,128)(2,1)S(1)}, bf16[10,1,16,256]{3,2,1,0:T(8,128)(2,1)S(1)}, u32[]{:S(2)}, u32[]{:S(2)}) collective-permute-start(bf16[10,1,16,256]{3,2,1,0:T(8,128)(2,1)S(1)} %get-tuple-element.70), channel_id=1, source_target_pairs={{0,32},{16,48},{32,64},{48,80},{64,96},{80,112},{96,128},{112,144}... | collective-permute-start | bytes 245768 | tf_op jit(solution)/shard_map/ppermute | solution.py:14
  172.5 6.0 %collective-permute-start.3 = (bf16[10,1,16,256]{3,2,1,0:T(8,128)(2,1)S(1)}, bf16[10,1,16,256]{3,2,1,0:T(8,128)(2,1)S(1)}, u32[]{:S(2)}, u32[]{:S(2)}) collective-permute-start(bf16[10,1,16,256]{3,2,1,0:T(8,128)(2,1)S(1)} %get-tuple-element.71), channel_id=1, source_target_pairs={{32,0},{48,16},{64,32},{80,48},{96,64},{112,80},{128,96},{144,112}... | collective-permute-start | bytes 245768 | tf_op jit(solution)/shard_map/ppermute | solution.py:14
  179.5 4.6 %collective-permute-done.3 = bf16[10,1,16,256]{3,2,1,0:T(8,128)(2,1)S(1)} collective-permute-done((bf16[10,1,16,256]{3,2,1,0:T(8,128)(2,1)S(1)}, bf16[10,1,16,256]{3,2,1,0:T(8,128)(2,1)S(1)}, u32[]{:S(2)}, u32[]{:S(2)}) %collective-permute-start.3) | collective-permute-done | bytes 81952 | tf_op jit(solution)/shard_map/ppermute | solution.py:14
  184.2 6.7 %collective-permute-start.5 = (bf16[10,6,1,256]{3,2,1,0:T(2,128)(2,1)S(1)}, bf16[10,6,1,256]{3,2,1,0:T(2,128)(2,1)S(1)}, u32[]{:S(2)}, u32[]{:S(2)}) collective-permute-start(bf16[10,6,1,256]{3,2,1,0:T(2,128)(2,1)S(1)} %get-tuple-element.48), channel_id=1, source_target_pairs={{16,0},{32,16},{48,32},{64,48},{80,64},{96,80},{112,96},{128,112},... | collective-permute-start | bytes 92168 | tf_op jit(solution)/shard_map/ppermute | solution.py:14
  190.8 1.9 collective-permute-start.4
  194.0 7.2 %collective-permute-done.4 = bf16[10,6,1,256]{3,2,1,0:T(2,128)(2,1)S(1)} collective-permute-done((bf16[10,6,1,256]{3,2,1,0:T(2,128)(2,1)S(1)}, bf16[10,6,1,256]{3,2,1,0:T(2,128)(2,1)S(1)}, u32[]{:S(2)}, u32[]{:S(2)}) %collective-permute-start.4) | collective-permute-done | bytes 30752 | tf_op jit(solution)/shard_map/ppermute | solution.py:14
  201.7 1.9 fusion.67
  207.6 127.3 %all-gather.11.cloned.1.call-done = bf16[2,6912,256]{2,1,0:T(8,128)(2,1)} async-done(((bf16[2,216,256]{2,1,0:T(8,128)(2,1)}), bf16[2,6912,256]{2,1,0:T(8,128)(2,1)}) %all-gather.11.cloned.1.call-update) | async-done | bytes 7077904 | tf_op jit(solution)/shard_map/all_gather | solution.py:107
  352.7 4.8 %collective-permute-start.6 = (bf16[1,4,16,256]{3,2,1,0:T(8,128)(2,1)S(1)}, bf16[1,4,16,256]{3,2,1,0:T(8,128)(2,1)S(1)}, u32[]{:S(2)}, u32[]{:S(2)}) collective-permute-start(bf16[1,4,16,256]{3,2,1,0:T(8,128)(2,1)S(1)} %get-tuple-element.74), channel_id=1, source_target_pairs={{0,64},{16,80},{32,96},{48,112},{64,128},{80,144},{96,160},{112,17... | collective-permute-start | bytes 98312 | tf_op jit(solution)/shard_map/ppermute | solution.py:14
  358.3 7.3 %collective-permute-start.7 = (bf16[1,4,16,256]{3,2,1,0:T(8,128)(2,1)S(1)}, bf16[1,4,16,256]{3,2,1,0:T(8,128)(2,1)S(1)}, u32[]{:S(2)}, u32[]{:S(2)}) collective-permute-start(bf16[1,4,16,256]{3,2,1,0:T(8,128)(2,1)S(1)} %get-tuple-element.75), channel_id=1, source_target_pairs={{64,0},{80,16},{96,32},{112,48},{128,64},{144,80},{160,96},{176,11... | collective-permute-start | bytes 98312 | tf_op jit(solution)/shard_map/ppermute | solution.py:14
  365.6 2.4 collective-permute-done.7
  368.0 4.0 collective-permute-start.8
  372.0 8.4 %collective-permute-start.9 = (bf16[10,1,16,256]{3,2,1,0:T(8,128)(2,1)S(1)}, bf16[10,1,16,256]{3,2,1,0:T(8,128)(2,1)S(1)}, u32[]{:S(2)}, u32[]{:S(2)}) collective-permute-start(bf16[10,1,16,256]{3,2,1,0:T(8,128)(2,1)S(1)} %get-tuple-element.67), channel_id=1, source_target_pairs={{32,0},{48,16},{64,32},{80,48},{96,64},{112,80},{128,96},{144,112}... | collective-permute-start | bytes 245768 | tf_op jit(solution)/shard_map/ppermute | solution.py:14
  380.9 1.9 collective-permute-done.9
  383.1 7.1 %collective-permute-start.11 = (bf16[10,6,1,256]{3,2,1,0:T(2,128)(2,1)S(1)}, bf16[10,6,1,256]{3,2,1,0:T(2,128)(2,1)S(1)}, u32[]{:S(2)}, u32[]{:S(2)}) collective-permute-start(bf16[10,6,1,256]{3,2,1,0:T(2,128)(2,1)S(1)} %get-tuple-element.44), channel_id=1, source_target_pairs={{16,0},{32,16},{48,32},{64,48},{80,64},{96,80},{112,96},{128,112},... | collective-permute-start | bytes 92168 | tf_op jit(solution)/shard_map/ppermute | solution.py:14
  390.2 2.1 collective-permute-start.10
  392.6 7.4 %collective-permute-done.10 = bf16[10,6,1,256]{3,2,1,0:T(2,128)(2,1)S(1)} collective-permute-done((bf16[10,6,1,256]{3,2,1,0:T(2,128)(2,1)S(1)}, bf16[10,6,1,256]{3,2,1,0:T(2,128)(2,1)S(1)}, u32[]{:S(2)}, u32[]{:S(2)}) %collective-permute-start.10) | collective-permute-done | bytes 30752 | tf_op jit(solution)/shard_map/ppermute | solution.py:14
  (148 shorter events, 42.1 us)
Async XLA Ops:
  7.2 143.1 %copy-start = (bf16[1,1,8,4,16,256]{5,4,3,2,1,0:T(8,128)(2,1)S(1)}, bf16[1,1,8,4,16,256]{5,4,3,2,1,0:T(8,128)(2,1)}, u32[]{:S(2)}) copy-start(bf16[1,1,8,4,16,256]{5,4,3,2,1,0:T(8,128)(2,1)} %param.6) | copy-start | bytes 786436
  7.2 50.9 %all-gather.5.cloned.1.call-start = ((), (), s32[]{:S(2)}) async-start(), calls=%async_computation | async-start | bytes 3760128 | tf_op jit(solution)/shard_map/all_gather | solution.py:18
  7.9 96.7 %all-gather.9.cloned.1.call-start = ((), (), s32[]{:S(2)}) async-start(), calls=%async_computation.2 | async-start | bytes 1880064 | tf_op jit(solution)/shard_map/all_gather | solution.py:23
  63.0 85.6 %all-gather.7.cloned.1.call-start = ((), (), s32[]{:S(2)}) async-start(), calls=%async_computation.1 | async-start | bytes 1880064 | tf_op jit(solution)/shard_map/all_gather | solution.py:23
  63.8 271.1 %all-gather.11.cloned.1.call-start = ((), (), s32[]{:S(2)}) async-start(), calls=%async_computation.3 | async-start | bytes 7299072 | tf_op jit(solution)/shard_map/all_gather | solution.py:107
  150.3 12.3 %collective-permute-start = (bf16[1,4,16,256]{3,2,1,0:T(8,128)(2,1)S(1)}, bf16[1,4,16,256]{3,2,1,0:T(8,128)(2,1)S(1)}, u32[]{:S(2)}, u32[]{:S(2)}) collective-permute-start(bf16[1,4,16,256]{3,2,1,0:T(8,128)(2,1)S(1)} %get-tuple-element.78), channel_id=1, source_target_pairs={{0,64},{16,80},{32,96},{48,112},{64,128},{80,144},{96,160},{112,17... | collective-permute-start | bytes 98312 | tf_op jit(solution)/shard_map/ppermute | solution.py:14
  158.0 10.1 %collective-permute-start.1 = (bf16[1,4,16,256]{3,2,1,0:T(8,128)(2,1)S(1)}, bf16[1,4,16,256]{3,2,1,0:T(8,128)(2,1)S(1)}, u32[]{:S(2)}, u32[]{:S(2)}) collective-permute-start(bf16[1,4,16,256]{3,2,1,0:T(8,128)(2,1)S(1)} %get-tuple-element.79), channel_id=1, source_target_pairs={{64,0},{80,16},{96,32},{112,48},{128,64},{144,80},{160,96},{176,11... | collective-permute-start | bytes 98312 | tf_op jit(solution)/shard_map/ppermute | solution.py:14
  168.1 11.3 %collective-permute-start.2 = (bf16[10,1,16,256]{3,2,1,0:T(8,128)(2,1)S(1)}, bf16[10,1,16,256]{3,2,1,0:T(8,128)(2,1)S(1)}, u32[]{:S(2)}, u32[]{:S(2)}) collective-permute-start(bf16[10,1,16,256]{3,2,1,0:T(8,128)(2,1)S(1)} %get-tuple-element.70), channel_id=1, source_target_pairs={{0,32},{16,48},{32,64},{48,80},{64,96},{80,112},{96,128},{112,144}... | collective-permute-start | bytes 245768 | tf_op jit(solution)/shard_map/ppermute | solution.py:14
  172.5 11.6 %collective-permute-start.3 = (bf16[10,1,16,256]{3,2,1,0:T(8,128)(2,1)S(1)}, bf16[10,1,16,256]{3,2,1,0:T(8,128)(2,1)S(1)}, u32[]{:S(2)}, u32[]{:S(2)}) collective-permute-start(bf16[10,1,16,256]{3,2,1,0:T(8,128)(2,1)S(1)} %get-tuple-element.71), channel_id=1, source_target_pairs={{32,0},{48,16},{64,32},{80,48},{96,64},{112,80},{128,96},{144,112}... | collective-permute-start | bytes 245768 | tf_op jit(solution)/shard_map/ppermute | solution.py:14
  184.2 9.7 %collective-permute-start.5 = (bf16[10,6,1,256]{3,2,1,0:T(2,128)(2,1)S(1)}, bf16[10,6,1,256]{3,2,1,0:T(2,128)(2,1)S(1)}, u32[]{:S(2)}, u32[]{:S(2)}) collective-permute-start(bf16[10,6,1,256]{3,2,1,0:T(2,128)(2,1)S(1)} %get-tuple-element.48), channel_id=1, source_target_pairs={{16,0},{32,16},{48,32},{64,48},{80,64},{96,80},{112,96},{128,112},... | collective-permute-start | bytes 92168 | tf_op jit(solution)/shard_map/ppermute | solution.py:14
  190.8 10.3 %collective-permute-start.4 = (bf16[10,6,1,256]{3,2,1,0:T(2,128)(2,1)S(1)}, bf16[10,6,1,256]{3,2,1,0:T(2,128)(2,1)S(1)}, u32[]{:S(2)}, u32[]{:S(2)}) collective-permute-start(bf16[10,6,1,256]{3,2,1,0:T(2,128)(2,1)S(1)} %get-tuple-element.49), channel_id=1, source_target_pairs={{0,16},{16,32},{32,48},{48,64},{64,80},{80,96},{96,112},{112,128},... | collective-permute-start | bytes 92168 | tf_op jit(solution)/shard_map/ppermute | solution.py:14
  192.9 10.7 %copy-start.2 = (f32[1,2,216,256]{3,2,1,0:T(8,128)S(1)}, f32[1,2,216,256]{3,2,1,0:T(8,128)}, u32[]{:S(2)}) copy-start(f32[1,2,216,256]{3,2,1,0:T(8,128)} %param.10) | copy-start | bytes 1327108
  192.9 10.7 %copy-start.3 = (f32[1,2,216,256]{3,2,1,0:T(8,128)S(1)}, f32[1,2,216,256]{3,2,1,0:T(8,128)}, u32[]{:S(2)}) copy-start(f32[1,2,216,256]{3,2,1,0:T(8,128)} %param.9) | copy-start | bytes 1327108
  207.6 141.4 %copy-start.14 = (bf16[8,4,16,256]{3,2,1,0:T(8,128)(2,1)S(1)}, bf16[8,4,16,256]{3,2,1,0:T(8,128)(2,1)}, u32[]{:S(2)}) copy-start(bf16[8,4,16,256]{3,2,1,0:T(8,128)(2,1)} %get-tuple-element.31) | copy-start | bytes 786436
  334.9 10.0 %copy-start.1 = (bf16[2,6912,256]{2,1,0:T(8,128)(2,1)S(1)}, bf16[2,6912,256]{2,1,0:T(8,128)(2,1)}, u32[]{:S(2)}) copy-start(bf16[2,6912,256]{2,1,0:T(8,128)(2,1)} %all-gather.11.cloned.1.call-done) | copy-start | bytes 21233668
  334.9 11.4 %copy-start.15 = (bf16[8,4,16,256]{3,2,1,0:T(8,128)(2,1)S(1)}, bf16[8,4,16,256]{3,2,1,0:T(8,128)(2,1)}, u32[]{:S(2)}) copy-start(bf16[8,4,16,256]{3,2,1,0:T(8,128)(2,1)} %get-tuple-element.32) | copy-start | bytes 786436
  336.2 13.0 %copy-start.13 = (bf16[8,4,16,256]{3,2,1,0:T(8,128)(2,1)S(1)}, bf16[8,4,16,256]{3,2,1,0:T(8,128)(2,1)}, u32[]{:S(2)}) copy-start(bf16[8,4,16,256]{3,2,1,0:T(8,128)(2,1)} %get-tuple-element.86) | copy-start | bytes 786436
  339.0 10.4 %copy-start.5 = (bf16[8,4,16,256]{3,2,1,0:T(8,128)(2,1)S(1)}, bf16[8,4,16,256]{3,2,1,0:T(8,128)(2,1)}, u32[]{:S(2)}) copy-start(bf16[8,4,16,256]{3,2,1,0:T(8,128)(2,1)} %get-tuple-element.60) | copy-start | bytes 786436
  352.7 12.9 %collective-permute-start.6 = (bf16[1,4,16,256]{3,2,1,0:T(8,128)(2,1)S(1)}, bf16[1,4,16,256]{3,2,1,0:T(8,128)(2,1)S(1)}, u32[]{:S(2)}, u32[]{:S(2)}) collective-permute-start(bf16[1,4,16,256]{3,2,1,0:T(8,128)(2,1)S(1)} %get-tuple-element.74), channel_id=1, source_target_pairs={{0,64},{16,80},{32,96},{48,112},{64,128},{80,144},{96,160},{112,17... | collective-permute-start | bytes 98312 | tf_op jit(solution)/shard_map/ppermute | solution.py:14
  358.3 9.7 %collective-permute-start.7 = (bf16[1,4,16,256]{3,2,1,0:T(8,128)(2,1)S(1)}, bf16[1,4,16,256]{3,2,1,0:T(8,128)(2,1)S(1)}, u32[]{:S(2)}, u32[]{:S(2)}) collective-permute-start(bf16[1,4,16,256]{3,2,1,0:T(8,128)(2,1)S(1)} %get-tuple-element.75), channel_id=1, source_target_pairs={{64,0},{80,16},{96,32},{112,48},{128,64},{144,80},{160,96},{176,11... | collective-permute-start | bytes 98312 | tf_op jit(solution)/shard_map/ppermute | solution.py:14
  368.0 12.9 %collective-permute-start.8 = (bf16[10,1,16,256]{3,2,1,0:T(8,128)(2,1)S(1)}, bf16[10,1,16,256]{3,2,1,0:T(8,128)(2,1)S(1)}, u32[]{:S(2)}, u32[]{:S(2)}) collective-permute-start(bf16[10,1,16,256]{3,2,1,0:T(8,128)(2,1)S(1)} %get-tuple-element.66), channel_id=1, source_target_pairs={{0,32},{16,48},{32,64},{48,80},{64,96},{80,112},{96,128},{112,144}... | collective-permute-start | bytes 245768 | tf_op jit(solution)/shard_map/ppermute | solution.py:14
  372.0 10.8 %collective-permute-start.9 = (bf16[10,1,16,256]{3,2,1,0:T(8,128)(2,1)S(1)}, bf16[10,1,16,256]{3,2,1,0:T(8,128)(2,1)S(1)}, u32[]{:S(2)}, u32[]{:S(2)}) collective-permute-start(bf16[10,1,16,256]{3,2,1,0:T(8,128)(2,1)S(1)} %get-tuple-element.67), channel_id=1, source_target_pairs={{32,0},{48,16},{64,32},{80,48},{96,64},{112,80},{128,96},{144,112}... | collective-permute-start | bytes 245768 | tf_op jit(solution)/shard_map/ppermute | solution.py:14
  383.1 9.4 %collective-permute-start.11 = (bf16[10,6,1,256]{3,2,1,0:T(2,128)(2,1)S(1)}, bf16[10,6,1,256]{3,2,1,0:T(2,128)(2,1)S(1)}, u32[]{:S(2)}, u32[]{:S(2)}) collective-permute-start(bf16[10,6,1,256]{3,2,1,0:T(2,128)(2,1)S(1)} %get-tuple-element.44), channel_id=1, source_target_pairs={{16,0},{32,16},{48,32},{64,48},{80,64},{96,80},{112,96},{128,112},... | collective-permute-start | bytes 92168 | tf_op jit(solution)/shard_map/ppermute | solution.py:14
  390.2 9.7 %collective-permute-start.10 = (bf16[10,6,1,256]{3,2,1,0:T(2,128)(2,1)S(1)}, bf16[10,6,1,256]{3,2,1,0:T(2,128)(2,1)S(1)}, u32[]{:S(2)}, u32[]{:S(2)}) collective-permute-start(bf16[10,6,1,256]{3,2,1,0:T(2,128)(2,1)S(1)} %get-tuple-element.45), channel_id=1, source_target_pairs={{0,16},{16,32},{32,48},{48,64},{64,80},{80,96},{96,112},{112,128},... | collective-permute-start | bytes 92168 | tf_op jit(solution)/shard_map/ppermute | solution.py:14
  (10 other events, 44.9 us)
Sparse Core Ops, SparseCore 0:
  10.1 47.9 all-gather.4
  63.2 41.4 all-gather.8
  107.4 41.2 all-gather.6
  151.6 183.2 all-gather.10
where the time goes:
time: 416 us; the launch traced here: 415 us
  waiting for transfers between devices  287 us (69%)
  starting transfers between devices  65 us (16%)
  matrix products  23.4 us (6%)
  between operations  18.6 us (4%)
  other arithmetic  11.2 us (3%)
  local copies, waits for them, and re-layouts  9.75 us (2%)
    all_gather x1, waiting for transfers between devices, shards(): lax.all_gather(new_master.astype(jnp.bfloat16), 'space', axis=1, tiled=True)  127 us
    all_gather x2, waiting for transfers between devices, from_root(): lax.all_gather(array, axis)  78.7 us
    ppermute x12, starting transfers between devices, passed_along(): lax.ppermute(value, axis, [(source, source + steps) for source in range(f...  64.9 us
    all_gather x1, waiting for transfers between devices, over_pieces(): blocks = lax.all_gather(array, axis).astype(jnp.float32)  50.1 us
    ppermute x12, waiting for transfers between devices, passed_along(): lax.ppermute(value, axis, [(source, source + steps) for source in range(f...  29.5 us
    dot_general x54, matrix products, convolve(): jnp.dot(window.reshape(-1, channels), weights_tap, preferred_element_type...  23.4 us
  transfers between devices with their start and end apart: 16, of which 12 were waited for; matrix products, arithmetic and copies ran while one was open for 3% of the time, Pallas kernels for 0%

commit v1 on v0

--- a/solution.py
+++ b/solution.py
@@ -104,7 +104,12 @@
     new_weights = lax.dynamic_slice_in_dim(
         new_master.reshape(filter_count, -1), rep_pos * share_len, share_len, 1
     )
-    filters = lax.all_gather(new_master.astype(jnp.bfloat16), "space", axis=1, tiled=True)
+    filters = jnp.concatenate(
+        lax.all_to_all(
+            jnp.stack([new_master.astype(jnp.bfloat16)] * lax.axis_size("space")), "space", 0, 0
+        ),
+        axis=1,
+    )
     grid = (lax.axis_size("space") // (GY * GZ), GY, GZ)
     strides = (GY * GZ, GZ, 1)
     coords = (space_pos // (GY * GZ), space_pos // GZ % GY, space_pos % GZ)

time: 416 us -> 581 us (1.40)
  waiting for transfers between devices: 287 us -> 446 us
  starting transfers between devices: 65 us -> 77.2 us
  matrix products: 23.4 us -> 12.5 us
  local copies, waits for them, and re-layouts: 9.75 us -> 16.5 us
    ppermute x12, waiting for transfers between devices: 29.5 us -> 316 us  [passed_along(): lax.ppermute(value, axis, [(source, source + steps) for source in range(f...]
    all_gather x1 -> x0, waiting for transfers between devices: 127 us -> none  [shards(): lax.all_gather(new_master.astype(jnp.bfloat16), 'space', axis=1, tiled=True)]
    all_to_all x0 -> x1, starting transfers between devices: none -> 15.5 us  [shards(): lax.all_to_all(jnp.stack([new_master.astype(jnp.bfloat16)] * lax.axis_siz...]
    dot_general x54, matrix products: 23.4 us -> 12.5 us  [convolve(): jnp.dot(window.reshape(-1, channels), weights_tap, preferred_element_type...]
  transfers between devices with their start and end apart: 16 -> 16, of which waited for: 12 -> 10; matrix products, arithmetic and copies ran while one was open for 3% -> 2% of each run, Pallas kernels for 0% -> 0%
where the time goes in v1:
time: 581 us; the launch traced here: 580 us
  waiting for transfers between devices  446 us (77%)
  starting transfers between devices  77.2 us (13%)
  between operations  18.7 us (3%)
  local copies, waits for them, and re-layouts  16.5 us (3%)
  matrix products  12.5 us (2%)
  other arithmetic  8.51 us (1%)
    ppermute x12, waiting for transfers between devices, passed_along(): lax.ppermute(value, axis, [(source, source + steps) for source in range(f...  316 us
    all_gather x2, waiting for transfers between devices, from_root(): lax.all_gather(array, axis)  79.4 us
    ppermute x12, starting transfers between devices, passed_along(): lax.ppermute(value, axis, [(source, source + steps) for source in range(f...  61.6 us
    all_gather x1, waiting for transfers between devices, over_pieces(): blocks = lax.all_gather(array, axis).astype(jnp.float32)  50.1 us
    all_to_all x1, starting transfers between devices, shards(): lax.all_to_all(jnp.stack([new_master.astype(jnp.bfloat16)] * lax.axis_siz...  15.5 us
    dot_general x54, matrix products, convolve(): jnp.dot(window.reshape(-1, channels), weights_tap, preferred_element_type...  12.5 us
  transfers between devices with their start and end apart: 16, of which 10 were waited for; matrix products, arithmetic and copies ran while one was open for 2% of the time, Pallas kernels for 0%

profile of v1, /device:TPU:24, one launch (start us, length us, event | category | flops | bytes accessed | tf_op | source)
XLA Modules:
  0.0 579.8 jit_solution(18402464837521828081)
XLA Ops:
  8.0 50.1 %all-gather.4.cloned.1.call-done = bf16[16,2,216,256]{3,2,1,0:T(8,128)(2,1)} async-done(((bf16[1,2,216,256]{3,2,1,0:T(8,128)(2,1)}), bf16[16,2,216,256]{3,2,1,0:T(8,128)(2,1)}) %all-gather.4.cloned.1.call-update) | async-done | bytes 3538960 | tf_op jit(solution)/shard_map/all_gather | solution.py:18
  58.1 2.6 convert_reduce_fusion
  67.2 36.3 %all-gather.8.cloned.1.call-done = bf16[16,216,256]{2,1,0:T(8,128)(2,1)} async-done(((bf16[1,216,256]{2,1,0:T(8,128)(2,1)}), bf16[16,216,256]{2,1,0:T(8,128)(2,1)}) %all-gather.8.cloned.1.call-update) | async-done | bytes 1769488 | tf_op jit(solution)/shard_map/all_gather | solution.py:23
  104.4 43.1 %all-gather.6.cloned.1.call-done = bf16[16,216,256]{2,1,0:T(8,128)(2,1)} async-done(((bf16[1,216,256]{2,1,0:T(8,128)(2,1)}), bf16[16,216,256]{2,1,0:T(8,128)(2,1)}) %all-gather.6.cloned.1.call-update) | async-done | bytes 1769488 | tf_op jit(solution)/shard_map/all_gather | solution.py:23
  148.4 3.4 stack.13
  151.8 15.5 %all-to-all-start = ((bf16[32,2,216,256]{3,2,1,0:T(8,128)(2,1)}), bf16[32,2,216,256]{3,2,1,0:T(8,128)(2,1)}, u32[]{:S(2)}, u32[]{:S(2)}) async-start(bf16[32,2,216,256]{3,2,1,0:T(8,128)(2,1)} %stack.13), calls=%async_computation | async-start | bytes 14155776 | tf_op jit(solution)/shard_map/all_to_all | solution.py:108
  167.3 7.3 %collective-permute-start = (bf16[1,4,16,256]{3,2,1,0:T(8,128)(2,1)S(1)}, bf16[1,4,16,256]{3,2,1,0:T(8,128)(2,1)S(1)}, u32[]{:S(2)}, u32[]{:S(2)}) collective-permute-start(bf16[1,4,16,256]{3,2,1,0:T(8,128)(2,1)S(1)} %get-tuple-element.80), channel_id=1, source_target_pairs={{0,64},{16,80},{32,96},{48,112},{64,128},{80,144},{96,160},{112,17... | collective-permute-start | bytes 98312 | tf_op jit(solution)/shard_map/ppermute | solution.py:14
  174.6 4.9 collective-permute-start.1
  179.5 293.9 %collective-permute-done = bf16[1,4,16,256]{3,2,1,0:T(8,128)(2,1)S(1)} collective-permute-done((bf16[1,4,16,256]{3,2,1,0:T(8,128)(2,1)S(1)}, bf16[1,4,16,256]{3,2,1,0:T(8,128)(2,1)S(1)}, u32[]{:S(2)}, u32[]{:S(2)}) %collective-permute-start) | collective-permute-done | bytes 32800 | tf_op jit(solution)/shard_map/ppermute | solution.py:14
  473.4 8.0 %collective-permute-start.2 = (bf16[10,1,16,256]{3,2,1,0:T(8,128)(2,1)S(1)}, bf16[10,1,16,256]{3,2,1,0:T(8,128)(2,1)S(1)}, u32[]{:S(2)}, u32[]{:S(2)}) collective-permute-start(bf16[10,1,16,256]{3,2,1,0:T(8,128)(2,1)S(1)} %get-tuple-element.72), channel_id=1, source_target_pairs={{0,32},{16,48},{32,64},{48,80},{64,96},{80,112},{96,128},{112,144}... | collective-permute-start | bytes 245768 | tf_op jit(solution)/shard_map/ppermute | solution.py:14
  481.4 2.9 collective-permute-start.3
  485.2 4.2 collective-permute-done.3
  489.5 8.1 %collective-permute-start.5 = (bf16[10,6,1,256]{3,2,1,0:T(2,128)(2,1)S(1)}, bf16[10,6,1,256]{3,2,1,0:T(2,128)(2,1)S(1)}, u32[]{:S(2)}, u32[]{:S(2)}) collective-permute-start(bf16[10,6,1,256]{3,2,1,0:T(2,128)(2,1)S(1)} %get-tuple-element.50), channel_id=1, source_target_pairs={{16,0},{32,16},{48,32},{64,48},{80,64},{96,80},{112,96},{128,112},... | collective-permute-start | bytes 92168 | tf_op jit(solution)/shard_map/ppermute | solution.py:14
  497.6 1.9 collective-permute-start.4
  500.8 6.6 %collective-permute-done.4 = bf16[10,6,1,256]{3,2,1,0:T(2,128)(2,1)S(1)} collective-permute-done((bf16[10,6,1,256]{3,2,1,0:T(2,128)(2,1)S(1)}, bf16[10,6,1,256]{3,2,1,0:T(2,128)(2,1)S(1)}, u32[]{:S(2)}, u32[]{:S(2)}) %collective-permute-start.4) | collective-permute-done | bytes 30752 | tf_op jit(solution)/shard_map/ppermute | solution.py:14
  507.9 2.0 fusion.122
  513.1 3.6 fusion.119
  524.0 1.9 collective-permute-start.6
  526.6 10.2 %collective-permute-start.7 = (bf16[1,4,16,256]{3,2,1,0:T(8,128)(2,1)S(1)}, bf16[1,4,16,256]{3,2,1,0:T(8,128)(2,1)S(1)}, u32[]{:S(2)}, u32[]{:S(2)}) collective-permute-start(bf16[1,4,16,256]{3,2,1,0:T(8,128)(2,1)S(1)} %get-tuple-element.77), channel_id=1, source_target_pairs={{64,0},{80,16},{96,32},{112,48},{128,64},{144,80},{160,96},{176,11... | collective-permute-start | bytes 98312 | tf_op jit(solution)/shard_map/ppermute | solution.py:14
  538.4 1.9 collective-permute-start.8
  540.4 8.4 %collective-permute-start.9 = (bf16[10,1,16,256]{3,2,1,0:T(8,128)(2,1)S(1)}, bf16[10,1,16,256]{3,2,1,0:T(8,128)(2,1)S(1)}, u32[]{:S(2)}, u32[]{:S(2)}) collective-permute-start(bf16[10,1,16,256]{3,2,1,0:T(8,128)(2,1)S(1)} %get-tuple-element.69), channel_id=1, source_target_pairs={{32,0},{48,16},{64,32},{80,48},{96,64},{112,80},{128,96},{144,112}... | collective-permute-start | bytes 245768 | tf_op jit(solution)/shard_map/ppermute | solution.py:14
  551.2 3.7 collective-permute-start.11
  554.9 2.3 collective-permute-start.10
  557.5 7.3 %collective-permute-done.10 = bf16[10,6,1,256]{3,2,1,0:T(2,128)(2,1)S(1)} collective-permute-done((bf16[10,6,1,256]{3,2,1,0:T(2,128)(2,1)S(1)}, bf16[10,6,1,256]{3,2,1,0:T(2,128)(2,1)S(1)}, u32[]{:S(2)}, u32[]{:S(2)}) %collective-permute-start.10) | collective-permute-done | bytes 30752 | tf_op jit(solution)/shard_map/ppermute | solution.py:14
  (161 shorter events, 31.1 us)
Async XLA Ops:
  7.2 53.5 %copy-start.1 = (f32[1,2,216,256]{3,2,1,0:T(8,128)S(1)}, f32[1,2,216,256]{3,2,1,0:T(8,128)}, u32[]{:S(2)}) copy-start(f32[1,2,216,256]{3,2,1,0:T(8,128)} %param.10) | copy-start | bytes 1327108
  7.2 53.5 %copy-start.2 = (f32[1,2,216,256]{3,2,1,0:T(8,128)S(1)}, f32[1,2,216,256]{3,2,1,0:T(8,128)}, u32[]{:S(2)}) copy-start(f32[1,2,216,256]{3,2,1,0:T(8,128)} %param.9) | copy-start | bytes 1327108
  7.2 53.5 %copy-start.22 = (f32[2,216,256]{2,1,0:T(8,128)S(1)}, f32[2,216,256]{2,1,0:T(8,128)}, u32[]{:S(2)}) copy-start(f32[2,216,256]{2,1,0:T(8,128)} %param.8) | copy-start | bytes 1327108
  7.2 55.4 %copy-start.23 = (s32[2,32]{1,0:T(2,128)S(1)}, s32[2,32]{1,0:T(2,128)}, u32[]{:S(2)}) copy-start(s32[2,32]{1,0:T(2,128)} %param.11) | copy-start | bytes 772
  7.2 50.9 %all-gather.4.cloned.1.call-start = ((), (), s32[]{:S(2)}) async-start(), calls=%async_computation.1 | async-start | bytes 3760128 | tf_op jit(solution)/shard_map/all_gather | solution.py:18
  7.9 95.5 %all-gather.8.cloned.1.call-start = ((), (), s32[]{:S(2)}) async-start(), calls=%async_computation.3 | async-start | bytes 1880064 | tf_op jit(solution)/shard_map/all_gather | solution.py:23
  61.8 85.6 %all-gather.6.cloned.1.call-start = ((), (), s32[]{:S(2)}) async-start(), calls=%async_computation.2 | async-start | bytes 1880064 | tf_op jit(solution)/shard_map/all_gather | solution.py:23
  151.8 15.5 %copy-start = (bf16[1,1,8,4,16,256]{5,4,3,2,1,0:T(8,128)(2,1)S(1)}, bf16[1,1,8,4,16,256]{5,4,3,2,1,0:T(8,128)(2,1)}, u32[]{:S(2)}) copy-start(bf16[1,1,8,4,16,256]{5,4,3,2,1,0:T(8,128)(2,1)} %param.6) | copy-start | bytes 786436
  151.8 361.3 %all-to-all-start = ((bf16[32,2,216,256]{3,2,1,0:T(8,128)(2,1)}), bf16[32,2,216,256]{3,2,1,0:T(8,128)(2,1)}, u32[]{:S(2)}, u32[]{:S(2)}) async-start(bf16[32,2,216,256]{3,2,1,0:T(8,128)(2,1)} %stack.13), calls=%async_computation | async-start | bytes 14155776 | tf_op jit(solution)/shard_map/all_to_all | solution.py:108
  167.3 306.1 %collective-permute-start = (bf16[1,4,16,256]{3,2,1,0:T(8,128)(2,1)S(1)}, bf16[1,4,16,256]{3,2,1,0:T(8,128)(2,1)S(1)}, u32[]{:S(2)}, u32[]{:S(2)}) collective-permute-start(bf16[1,4,16,256]{3,2,1,0:T(8,128)(2,1)S(1)} %get-tuple-element.80), channel_id=1, source_target_pairs={{0,64},{16,80},{32,96},{48,112},{64,128},{80,144},{96,160},{112,17... | collective-permute-start | bytes 98312 | tf_op jit(solution)/shard_map/ppermute | solution.py:14
  174.6 298.8 %collective-permute-start.1 = (bf16[1,4,16,256]{3,2,1,0:T(8,128)(2,1)S(1)}, bf16[1,4,16,256]{3,2,1,0:T(8,128)(2,1)S(1)}, u32[]{:S(2)}, u32[]{:S(2)}) collective-permute-start(bf16[1,4,16,256]{3,2,1,0:T(8,128)(2,1)S(1)} %get-tuple-element.81), channel_id=1, source_target_pairs={{64,0},{80,16},{96,32},{112,48},{128,64},{144,80},{160,96},{176,11... | collective-permute-start | bytes 98312 | tf_op jit(solution)/shard_map/ppermute | solution.py:14
  473.4 11.7 %collective-permute-start.2 = (bf16[10,1,16,256]{3,2,1,0:T(8,128)(2,1)S(1)}, bf16[10,1,16,256]{3,2,1,0:T(8,128)(2,1)S(1)}, u32[]{:S(2)}, u32[]{:S(2)}) collective-permute-start(bf16[10,1,16,256]{3,2,1,0:T(8,128)(2,1)S(1)} %get-tuple-element.72), channel_id=1, source_target_pairs={{0,32},{16,48},{32,64},{48,80},{64,96},{80,112},{96,128},{112,144}... | collective-permute-start | bytes 245768 | tf_op jit(solution)/shard_map/ppermute | solution.py:14
  481.4 7.9 %collective-permute-start.3 = (bf16[10,1,16,256]{3,2,1,0:T(8,128)(2,1)S(1)}, bf16[10,1,16,256]{3,2,1,0:T(8,128)(2,1)S(1)}, u32[]{:S(2)}, u32[]{:S(2)}) collective-permute-start(bf16[10,1,16,256]{3,2,1,0:T(8,128)(2,1)S(1)} %get-tuple-element.73), channel_id=1, source_target_pairs={{32,0},{48,16},{64,32},{80,48},{96,64},{112,80},{128,96},{144,112}... | collective-permute-start | bytes 245768 | tf_op jit(solution)/shard_map/ppermute | solution.py:14
  489.5 11.2 %collective-permute-start.5 = (bf16[10,6,1,256]{3,2,1,0:T(2,128)(2,1)S(1)}, bf16[10,6,1,256]{3,2,1,0:T(2,128)(2,1)S(1)}, u32[]{:S(2)}, u32[]{:S(2)}) collective-permute-start(bf16[10,6,1,256]{3,2,1,0:T(2,128)(2,1)S(1)} %get-tuple-element.50), channel_id=1, source_target_pairs={{16,0},{32,16},{48,32},{64,48},{80,64},{96,80},{112,96},{128,112},... | collective-permute-start | bytes 92168 | tf_op jit(solution)/shard_map/ppermute | solution.py:14
  497.6 9.7 %collective-permute-start.4 = (bf16[10,6,1,256]{3,2,1,0:T(2,128)(2,1)S(1)}, bf16[10,6,1,256]{3,2,1,0:T(2,128)(2,1)S(1)}, u32[]{:S(2)}, u32[]{:S(2)}) collective-permute-start(bf16[10,6,1,256]{3,2,1,0:T(2,128)(2,1)S(1)} %get-tuple-element.51), channel_id=1, source_target_pairs={{0,16},{16,32},{32,48},{48,64},{64,80},{80,96},{96,112},{112,128},... | collective-permute-start | bytes 92168 | tf_op jit(solution)/shard_map/ppermute | solution.py:14
  513.1 3.6 copy-start.4
  513.1 3.8 copy-start.3
  517.0 1.9 copy-start.11
  524.0 12.9 %collective-permute-start.6 = (bf16[1,4,16,256]{3,2,1,0:T(8,128)(2,1)S(1)}, bf16[1,4,16,256]{3,2,1,0:T(8,128)(2,1)S(1)}, u32[]{:S(2)}, u32[]{:S(2)}) collective-permute-start(bf16[1,4,16,256]{3,2,1,0:T(8,128)(2,1)S(1)} %get-tuple-element.76), channel_id=1, source_target_pairs={{0,64},{16,80},{32,96},{48,112},{64,128},{80,144},{96,160},{112,17... | collective-permute-start | bytes 98312 | tf_op jit(solution)/shard_map/ppermute | solution.py:14
  526.6 11.8 %collective-permute-start.7 = (bf16[1,4,16,256]{3,2,1,0:T(8,128)(2,1)S(1)}, bf16[1,4,16,256]{3,2,1,0:T(8,128)(2,1)S(1)}, u32[]{:S(2)}, u32[]{:S(2)}) collective-permute-start(bf16[1,4,16,256]{3,2,1,0:T(8,128)(2,1)S(1)} %get-tuple-element.77), channel_id=1, source_target_pairs={{64,0},{80,16},{96,32},{112,48},{128,64},{144,80},{160,96},{176,11... | collective-permute-start | bytes 98312 | tf_op jit(solution)/shard_map/ppermute | solution.py:14
  538.4 10.8 %collective-permute-start.8 = (bf16[10,1,16,256]{3,2,1,0:T(8,128)(2,1)S(1)}, bf16[10,1,16,256]{3,2,1,0:T(8,128)(2,1)S(1)}, u32[]{:S(2)}, u32[]{:S(2)}) collective-permute-start(bf16[10,1,16,256]{3,2,1,0:T(8,128)(2,1)S(1)} %get-tuple-element.68), channel_id=1, source_target_pairs={{0,32},{16,48},{32,64},{48,80},{64,96},{80,112},{96,128},{112,144}... | collective-permute-start | bytes 245768 | tf_op jit(solution)/shard_map/ppermute | solution.py:14
  540.4 10.6 %collective-permute-start.9 = (bf16[10,1,16,256]{3,2,1,0:T(8,128)(2,1)S(1)}, bf16[10,1,16,256]{3,2,1,0:T(8,128)(2,1)S(1)}, u32[]{:S(2)}, u32[]{:S(2)}) collective-permute-start(bf16[10,1,16,256]{3,2,1,0:T(8,128)(2,1)S(1)} %get-tuple-element.69), channel_id=1, source_target_pairs={{32,0},{48,16},{64,32},{80,48},{96,64},{112,80},{128,96},{144,112}... | collective-permute-start | bytes 245768 | tf_op jit(solution)/shard_map/ppermute | solution.py:14
  551.2 6.2 %collective-permute-start.11 = (bf16[10,6,1,256]{3,2,1,0:T(2,128)(2,1)S(1)}, bf16[10,6,1,256]{3,2,1,0:T(2,128)(2,1)S(1)}, u32[]{:S(2)}, u32[]{:S(2)}) collective-permute-start(bf16[10,6,1,256]{3,2,1,0:T(2,128)(2,1)S(1)} %get-tuple-element.46), channel_id=1, source_target_pairs={{16,0},{32,16},{48,32},{64,48},{80,64},{96,80},{112,96},{128,112},... | collective-permute-start | bytes 92168 | tf_op jit(solution)/shard_map/ppermute | solution.py:14
  554.9 9.8 %collective-permute-start.10 = (bf16[10,6,1,256]{3,2,1,0:T(2,128)(2,1)S(1)}, bf16[10,6,1,256]{3,2,1,0:T(2,128)(2,1)S(1)}, u32[]{:S(2)}, u32[]{:S(2)}) collective-permute-start(bf16[10,6,1,256]{3,2,1,0:T(2,128)(2,1)S(1)} %get-tuple-element.47), channel_id=1, source_target_pairs={{0,16},{16,32},{32,48},{48,64},{64,80},{80,96},{96,112},{112,128},... | collective-permute-start | bytes 92168 | tf_op jit(solution)/shard_map/ppermute | solution.py:14
  (16 other events, 20.2 us)
Sparse Core Ops, SparseCore 0:
  10.2 47.9 all-gather.3
  61.9 41.4 all-gather.7
  106.2 41.2 all-gather.5
